TPU v7x, 128 devices: a whole 4x4x4 slice. The times are simulated.
128 devices in a mesh: expert: 8 (over y, core), tensor: 16 (over z, x).
Axes of the slice: x: 4, y: 4, z: 4, core: 2. Of those that a mesh axis runs over, the one named last changes fastest.
Arguments:
- tokens: bfloat16 [4096, 4096], P(('expert', 'tensor')), may hold values from -6 to 6
- expert_ids: int32 [4096, 2], P(('expert', 'tensor')), may hold values from 0 to 15, as said below
- slots: int32 [4096, 2], P(('expert', 'tensor')), may hold values from 0 to 7, as said below
- combine_weights: float32 [4096, 2], P(('expert', 'tensor')), may hold values from 0.25 to 1
- big_gate: bfloat16 [8, 4096, 14336], P('expert', None, 'tensor'), may hold values from -0.09375 to 0.09375
- big_up: bfloat16 [8, 4096, 14336], P('expert', None, 'tensor'), may hold values from -0.09375 to 0.09375
- big_down: bfloat16 [8, 14336, 4096], P('expert', 'tensor'), may hold values from -0.046875 to 0.046875
- small_gate: bfloat16 [8, 4096, 1792], P('expert', 'tensor'), may hold values from -0.09375 to 0.09375
- small_up: bfloat16 [8, 4096, 1792], P('expert', 'tensor'), may hold values from -0.09375 to 0.09375
- small_down: bfloat16 [8, 1792, 4096], P('expert', None, 'tensor'), may hold values from -0.125 to 0.125
Outputs:
- mixed: bfloat16 [4096, 4096], P(('expert', 'tensor'))
Inputs may be any that keep to these rules, and one draw needn't show every extreme that they name: `expert_ids`: each token names two different experts; an id below 8 is the big expert of that group index, an id of 8 or more is the small expert of group index id - 8. In each aligned block of 32 rows (the rows of one device) no expert is named more than 8 times, and at least one expert, the same for all blocks, is named exactly 8 times in every block. Within each aligned block of 32 rows, the choices that name one expert hold distinct slots.
All inputs are finite; a program needn't handle non-finite values.
Results may differ from a plain program's by a relative error of at most 0.025.
Values may be sent and summed in bfloat16 or wider, within the bound.
A program may use at most 128 MiB of HBM per device.

v0:
```python
import jax
import jax.numpy as jnp
from jax import lax
from jax.sharding import PartitionSpec as P


def shards(
    tokens,
    expert_ids,
    slots,
    combine_weights,
    big_gate,
    big_up,
    big_down,
    small_gate,
    small_up,
    small_down,
):
    tok_rows, width = tokens.shape
    groups = lax.axis_size("expert")
    kinds = 2 * groups
    capacity = 2 * tok_rows // groups
    flat = expert_ids * capacity + slots
    positions = jnp.arange(kinds * capacity, dtype=jnp.int32)
    first_hot = (flat[None, :, 0] == positions[:, None]).astype(jnp.float32)
    second_hot = (flat[None, :, 1] == positions[:, None]).astype(jnp.float32)
    onehot = (first_hot + second_hot).astype(jnp.bfloat16)
    packed = jnp.dot(onehot, tokens, preferred_element_type=jnp.float32).astype(jnp.bfloat16)
    packed = packed.reshape(2, groups, capacity, width)
    received = lax.all_to_all(packed, "expert", split_axis=1, concat_axis=1, tiled=True)
    rows = lax.all_gather(
        received[0].reshape(groups * capacity, width), "tensor", axis=0, tiled=True
    )
    gate = jnp.dot(rows, big_gate[0], preferred_element_type=jnp.float32)
    up = jnp.dot(rows, big_up[0], preferred_element_type=jnp.float32)
    hidden = (jax.nn.silu(gate) * up).astype(jnp.bfloat16)
    partial_value = jnp.dot(hidden, big_down[0], preferred_element_type=jnp.float32)
    small_rows = received[1].reshape(groups * capacity, width)
    columns = lax.all_to_all(small_rows, "tensor", split_axis=1, concat_axis=0, tiled=True)
    gate_part = jnp.dot(columns, small_gate[0], preferred_element_type=jnp.float32)
    up_part = jnp.dot(columns, small_up[0], preferred_element_type=jnp.float32)
    gate_sum, up_sum = (
        lax.psum(gate_part.astype(jnp.bfloat16), "tensor").astype(jnp.float32),
        lax.psum(up_part.astype(jnp.bfloat16), "tensor").astype(jnp.float32),
    )
    small_act = (jax.nn.silu(gate_sum) * up_sum).astype(jnp.bfloat16)
    small_cols = jnp.dot(small_act, small_down[0], preferred_element_type=jnp.float32).astype(
        jnp.bfloat16
    )
    small_back = lax.all_to_all(small_cols, "tensor", split_axis=0, concat_axis=1, tiled=True)
    big_back = lax.psum_scatter(
        partial_value.astype(jnp.bfloat16), "tensor", scatter_dimension=0, tiled=True
    )
    outgoing = jnp.stack([big_back, small_back]).reshape(2, groups, capacity, width)
    home = lax.all_to_all(outgoing, "expert", split_axis=1, concat_axis=1, tiled=True).reshape(
        kinds * capacity, width
    )
    first = jnp.take(home, flat[:, 0], axis=0).astype(jnp.float32)
    second = jnp.take(home, flat[:, 1], axis=0).astype(jnp.float32)
    mixed = combine_weights[:, 0:1] * first + combine_weights[:, 1:2] * second
    return mixed.astype(jnp.bfloat16)


def solution(mesh):
    return jax.shard_map(
        shards,
        mesh=mesh,
        in_specs=(
            P(("expert", "tensor"), None),
            P(("expert", "tensor"), None),
            P(("expert", "tensor"), None),
            P(("expert", "tensor"), None),
            P("expert", None, "tensor"),
            P("expert", None, "tensor"),
            P("expert", "tensor", None),
            P("expert", "tensor", None),
            P("expert", "tensor", None),
            P("expert", None, "tensor"),
        ),
        out_specs=P(("expert", "tensor"), None),
        check_vma=False,
    )
```

profile of v0, /device:TPU:1, one launch (start us, length us, event | category | flops | bytes accessed | tf_op | source)
XLA Modules:
  0.0 359.9 jit_solution(860827384541931274)
XLA Ops:
  6.5 0.8 multiply_add_fusion
  7.3 1.4 convolution_convert_fusion.1
  8.8 20.8 %all_to_all.45 = bf16[2,8,8,4096]{3,2,0,1:T(8,128)(2,1)S(1)} all-to-all(bf16[2,8,8,4096]{3,2,0,1:T(8,128)(2,1)S(1)} %copy.15), channel_id=1, replica_groups=mesh['expert'=8,'tensor'=16] {'expert'}, dimensions={1} | all-to-all | bytes 2097152 | tf_op jit(solution)/shard_map/all_to_all | solution.py:30
  29.6 0.9 slice_bitcast_fusion
  30.9 17.7 %all_to_all.46 = bf16[64,16,256]{2,0,1:T(8,128)(2,1)S(1)} all-to-all(bf16[64,16,256]{2,0,1:T(8,128)(2,1)S(1)} %copy.16), channel_id=1, replica_groups=mesh['expert'=8,'tensor'=16] {'tensor'}, dimensions={1} | all-to-all | bytes 1048576 | tf_op jit(solution)/shard_map/all_to_all | solution.py:39
  48.6 2.9 convolution_convert_fusion.2
  51.5 3.0 convolution_convert_fusion.3
  54.6 0.2 reduce-scatter.2.cloned.1.call-start
  54.8 47.5 %all-gather.2.cloned.1.call-done = bf16[1024,4096]{1,0:T(8,128)(2,1)} async-done(((bf16[64,4096]{1,0:T(8,128)(2,1)}), bf16[1024,4096]{1,0:T(8,128)(2,1)}) %all-gather.2.cloned.1.call-update) | async-done | bytes 8388624 | tf_op jit(solution)/shard_map/all_gather | solution.py:31
  102.3 12.5 %fusion.5 = f32[1024,896]{1,0:T(8,128)S(1)} fusion(bf16[1024,4096]{1,0:T(8,128)(2,1)} %all-gather.2.cloned.1.call-done, bf16[1,4096,896]{2,1,0:T(8,128)(2,1)} %param.17), kind=kOutput, calls=%fused_computation.10 | convolution fusion | flops 7516192768 | bytes 19398656 | tf_op jit(solution)/shard_map/dot_general | solution.py:35
  114.8 12.1 %multiply_convert_fusion = bf16[1024,896]{1,0:T(8,128)(2,1)S(1)} fusion(f32[1024,896]{1,0:T(8,128)S(1)} %fusion.5, bf16[1024,4096]{1,0:T(8,128)(2,1)S(1)} %copy-done.4, bf16[1,4096,896]{2,1,0:T(8,128)(2,1)} %param.16), kind=kOutput, calls=%fused_computation.18 | convolution fusion | flops 7521697792 | bytes 21233664 | tf_op jit(solution)/shard_map/dot_general | solution.py:34
  127.0 11.1 %convolution_convert_fusion = bf16[1024,4096]{1,0:T(8,128)(2,1)} fusion(bf16[1024,896]{1,0:T(8,128)(2,1)S(1)} %multiply_convert_fusion, bf16[1,896,4096]{2,1,0:T(8,128)(2,1)S(1)} %bitcast.68), kind=kOutput, calls=%fused_computation.4 | convolution fusion | flops 7520387072 | bytes 17563648 | tf_op jit(solution)/shard_map/dot_general | solution.py:37
  138.1 99.3 %all-reduce.3.cloned.1.call-done = (bf16[1024,1792]{1,0:T(8,128)(2,1)}, bf16[1024,1792]{1,0:T(8,128)(2,1)}) async-done(((bf16[1024,1792]{1,0:T(8,128)(2,1)}, bf16[1024,1792]{1,0:T(8,128)(2,1)}), (bf16[1024,1792]{1,0:T(8,128)(2,1)}, bf16[1024,1792]{1,0:T(8,128)(2,1)})) %all-reduce.3.cloned.1.call-update) | async-done | bytes 7340048 | tf_op jit(solution)/shard_map/psum | solution.py:44
  237.4 5.5 %fusion.14 = bf16[1024,256]{1,0:T(8,128)(2,1)S(1)} fusion(bf16[1024,1792]{1,0:T(8,128)(2,1)} %get-tuple-element.6, bf16[1024,1792]{1,0:T(8,128)(2,1)} %get-tuple-element.7, bf16[1,1792,256]{2,1,0:T(8,128)(2,1)S(1)} %copy-done.5), kind=kOutput, calls=%fused_computation.20 | convolution fusion | flops 954466304 | bytes 8781824 | tf_op jit(solution)/shard_map/dot_general | solution.py:47
  243.0 17.9 %all_to_all.47 = bf16[16,64,256]{2,1,0:T(8,128)(2,1)S(1)} all-to-all(bf16[16,64,256]{2,1,0:T(8,128)(2,1)S(1)} %bitcast.65), channel_id=1, replica_groups=mesh['expert'=8,'tensor'=16] {'tensor'}, dimensions={0} | all-to-all | bytes 1048576 | tf_op jit(solution)/shard_map/all_to_all | solution.py:50
  260.8 0.3 copy.17
  261.1 0.2 stack.10
  261.4 66.2 %reduce-scatter.2.cloned.1.call-done = bf16[64,4096]{1,0:T(8,128)(2,1)} async-done(((bf16[1024,4096]{1,0:T(8,128)(2,1)}), bf16[64,4096]{1,0:T(8,128)(2,1)}) %reduce-scatter.2.cloned.1.call-update) | async-done | bytes 524304 | tf_op jit(solution)/shard_map/reduce_scatter | solution.py:51
  327.6 2.1 pad_maximum_fusion
  329.7 6.2 %all-to-all-start.3 = ((bf16[2,8,8,4096]{3,2,0,1:T(8,128)(2,1)}), bf16[2,8,8,4096]{3,2,0,1:T(8,128)(2,1)S(1)}, u32[]{:S(2)}, u32[]{:S(2)}) async-start(bf16[2,8,8,4096]{3,2,0,1:T(8,128)(2,1)} %pad_maximum_fusion), calls=%async_computation.4 | async-start | bytes 2097152 | tf_op jit(solution)/shard_map/all_to_all | solution.py:55
  335.9 15.1 %all-to-all-done.3 = bf16[2,8,8,4096]{3,2,0,1:T(8,128)(2,1)S(1)} async-done(((bf16[2,8,8,4096]{3,2,0,1:T(8,128)(2,1)}), bf16[2,8,8,4096]{3,2,0,1:T(8,128)(2,1)S(1)}, u32[]{:S(2)}, u32[]{:S(2)}) %all-to-all-start.3) | async-done | bytes 1048608 | tf_op jit(solution)/shard_map/all_to_all | solution.py:55
  351.1 0.7 gather_fusion
  351.8 0.7 gather_fusion.1
  352.5 0.9 add_convert_fusion
  (30 shorter events, 0.6 us)
Async XLA Ops:
  6.5 42.1 %copy-start = (bf16[1,256,1792]{2,1,0:T(8,128)(2,1)S(1)}, bf16[1,256,1792]{2,1,0:T(8,128)(2,1)}, u32[]{:S(2)}) copy-start(bf16[1,256,1792]{2,1,0:T(8,128)(2,1)} %param.20) | copy-start | bytes 2752516
  6.5 95.8 %all-gather.2.cloned.1.call-start = ((), (), s32[]{:S(2)}) async-start(), calls=%async_computation.5 | async-start | bytes 8912896 | tf_op jit(solution)/shard_map/all_gather | solution.py:31
  29.6 21.9 %copy-start.2 = (bf16[1,256,1792]{2,1,0:T(8,128)(2,1)S(1)}, bf16[1,256,1792]{2,1,0:T(8,128)(2,1)}, u32[]{:S(2)}) copy-start(bf16[1,256,1792]{2,1,0:T(8,128)(2,1)} %param.19) | copy-start | bytes 2752516
  30.5 206.9 %all-reduce.3.cloned.1.call-start = ((), (), s32[]{:S(2)}) async-start(), calls=%async_computation.7 | async-start | bytes 14680064 | tf_op jit(solution)/shard_map/psum | solution.py:44
  54.6 273.0 %reduce-scatter.2.cloned.1.call-start = ((), (), s32[]{:S(2)}) async-start(), calls=%async_computation.6 | async-start | bytes 8912896 | tf_op jit(solution)/shard_map/reduce_scatter | solution.py:51
  102.3 12.5 %copy-start.4 = (bf16[1024,4096]{1,0:T(8,128)(2,1)S(1)}, bf16[1024,4096]{1,0:T(8,128)(2,1)}, u32[]{:S(2)}) copy-start(bf16[1024,4096]{1,0:T(8,128)(2,1)} %all-gather.2.cloned.1.call-done) | copy-start | bytes 25165828
  102.3 24.6 %slice-start = ((s8[7340032]{0:T(1024)(128)(4,1)}), s8[4194304]{0:T(1024)(128)(4,1)S(1)}, s32[]{:S(2)}) async-start(s8[7340032]{0:T(1024)(128)(4,1)} %bitcast.67), calls=%async_computation.8 | async-start | bytes 8388608
  114.8 12.1 %slice-start.1 = ((s8[7340032]{0:T(1024)(128)(4,1)}), s8[3145728]{0:T(1024)(128)(4,1)S(1)}, s32[]{:S(2)}) async-start(s8[7340032]{0:T(1024)(128)(4,1)} %bitcast.67), calls=%async_computation.9 | async-start | bytes 6291456
  138.1 99.3 %copy-start.5 = (bf16[1,1792,256]{2,1,0:T(8,128)(2,1)S(1)}, bf16[1,1792,256]{2,1,0:T(8,128)(2,1)}, u32[]{:S(2)}) copy-start(bf16[1,1792,256]{2,1,0:T(8,128)(2,1)} %param.21) | copy-start | bytes 2752516
  242.9 93.0 %copy-start.3 = (f32[32,2]{0,1:T(2,128)S(1)}, f32[32,2]{0,1:T(2,128)}, u32[]{:S(2)}) copy-start(f32[32,2]{0,1:T(2,128)} %param.15) | copy-start | bytes 772
  243.0 110.5 %copy-start.1 = (bf16[1,256,1792]{2,1,0:T(8,128)(2,1)S(1)}, bf16[1,256,1792]{2,1,0:T(8,128)(2,1)}, u32[]{:S(2)}) copy-start(bf16[1,256,1792]{2,1,0:T(8,128)(2,1)} %param.20) | copy-start | bytes 2752516
  329.7 21.3 %all-to-all-start.3 = ((bf16[2,8,8,4096]{3,2,0,1:T(8,128)(2,1)}), bf16[2,8,8,4096]{3,2,0,1:T(8,128)(2,1)S(1)}, u32[]{:S(2)}, u32[]{:S(2)}) async-start(bf16[2,8,8,4096]{3,2,0,1:T(8,128)(2,1)} %pad_maximum_fusion), calls=%async_computation.4 | async-start | bytes 2097152 | tf_op jit(solution)/shard_map/all_to_all | solution.py:55
Sparse Core Ops, SparseCore 0:
  30.6 71.6 all-gather.1
  105.8 131.5 all-reduce.2
  241.2 86.2 reduce-scatter.1
where the time goes:
time: 360 us
  waiting for transfers between devices  228 us (63%)
  blocking collectives  56.4 us (16%)
  matrix products  48.5 us (13%)
  between operations  13.3 us (4%)
  starting transfers between devices  6.45 us (2%)
  other arithmetic  3.83 us (1%)
    psum x1, waiting for transfers between devices, shards(): lax.psum(up_part.astype(jnp.bfloat16), 'tensor').astype(jnp.float32)  99.3 us
    reduce_scatter x1, waiting for transfers between devices, shards(): lax.psum_scatter(partial_value.astype(jnp.bfloat16), 'tensor', scatter_di...  66.2 us
    all_gather x1, waiting for transfers between devices, shards(): lax.all_gather(received[0].reshape(groups * capacity, width), 'tensor', a...  47.5 us
    all_to_all x1, blocking collectives, shards(): lax.all_to_all(packed, 'expert', split_axis=1, concat_axis=1, tiled=True)  20.8 us
    all_to_all x1, blocking collectives, shards(): lax.all_to_all(small_cols, 'tensor', split_axis=0, concat_axis=1, tiled=T...  17.9 us
    all_to_all x1, blocking collectives, shards(): lax.all_to_all(small_rows, 'tensor', split_axis=1, concat_axis=0, tiled=T...  17.7 us
    all_to_all x1, waiting for transfers between devices, shards(): lax.all_to_all(outgoing, 'expert', split_axis=1, concat_axis=1, tiled=True)  15.1 us
    dot_general x1, matrix products, shards(): up = jnp.dot(rows, big_up[0], preferred_element_type=jnp.float32)  12.5 us
  transfers between devices with their start and end apart: 4, of which 4 were waited for; matrix products, arithmetic and copies ran while one was open for 13% of the time, Pallas kernels for 0%

commit v1 on v0

v1 whole, which is shorter than its diff:
```python
import functools

import jax
import jax.numpy as jnp
from jax import lax
from jax.experimental import pallas as pl
from jax.experimental.pallas import tpu as pltpu
from jax.sharding import PartitionSpec as P

F32, BF16 = jnp.float32, jnp.bfloat16
MESH = pl.DeviceIdType.MESH
TILE = 256
AXES = (("x", "z"), ("z", "x"))


def add_into(dst, parts, rows, width):
    step = min(width, 512)

    @pl.loop(0, width // step)
    def _(c):
        cols = pl.ds(pl.multiple_of(c * step, step), step)
        total = dst[:, cols].astype(F32)
        for part in parts:
            total += part[:, cols].astype(F32)
        dst[:, cols] = total.astype(BF16)


class Copies:
    def __init__(self, send, recv):
        self.send, self.recv, self.used = send, recv, 0

    def __call__(self, src, dst, device):
        k = self.used
        self.used += 1
        return pltpu.make_async_remote_copy(
            src_ref=src, dst_ref=dst, send_sem=self.send.at[k], recv_sem=self.recv.at[k],
            device_id=device, device_id_type=MESH,
        )


class Gather:
    def __init__(self, copies, neighbour, buf):
        self.c = c = {}
        for h, (first, second) in enumerate(AXES):
            def row(g, r, lo=0, n=32):
                return buf.at[g, pl.ds(128 * h + 32 * r + lo, n)]

            c[h, "a", 1] = copies(row(0, 0), row(0, 3), neighbour(first, 1))
            c[h, "a", 3] = copies(row(0, 0), row(0, 1), neighbour(first, 3))
            c[h, "f", 1] = copies(row(0, 3, 0, 16), row(0, 2, 0, 16), neighbour(first, 1))
            c[h, "f", 3] = copies(row(0, 1, 16, 16), row(0, 2, 16, 16), neighbour(first, 3))
            for r in range(4):
                c[h, "b", 1, r] = copies(row(0, r), row(3, r), neighbour(second, 1))
                c[h, "b", 3, r] = copies(row(0, r), row(1, r), neighbour(second, 3))
            for r in (0, 1):
                c[h, "g", 1, r] = copies(row(3, r), row(2, r), neighbour(second, 1))
            for r in (2, 3):
                c[h, "g", 3, r] = copies(row(1, r), row(2, r), neighbour(second, 3))

    def step(self, number):
        c = self.c
        for h in (0, 1):
            def go(*keys):
                for key in keys:
                    c[(h, *key)].start()

            def got(*keys):
                for key in keys:
                    c[(h, *key)].wait_recv()

            if number == 0:
                go(("a", 1), ("a", 3), ("b", 1, 0), ("b", 3, 0))
            elif number == 1:
                got(("a", 1))
                go(("f", 1), ("b", 1, 3), ("b", 3, 3))
                got(("a", 3))
                go(("f", 3), ("b", 1, 1), ("b", 3, 1))
            elif number == 2:
                got(("b", 1, 0))
                go(("g", 1, 0))
            elif number == 3:
                got(("f", 1), ("f", 3))
                go(("b", 1, 2), ("b", 3, 2))
            elif number == 4:
                got(("b", 1, 1))
                go(("g", 1, 1))
                got(("b", 3, 3))
                go(("g", 3, 3))
            elif number == 5:
                got(("b", 3, 2))
                go(("g", 3, 2))
            else:
                got(("b", 1, 2), ("b", 1, 3), ("b", 3, 0), ("b", 3, 1))
                got(("g", 1, 0), ("g", 1, 1), ("g", 3, 2), ("g", 3, 3))

    def sent(self):
        for copy in self.c.values():
            copy.wait_send()


class Scatter:
    def __init__(self, copies, neighbour, row, width, o, n, o2, n2):
        self.row, self.width = row, width
        self.o, self.n, self.o2, self.n2 = o, n, o2, n2
        self.c = c = {}
        for h, (second, first) in enumerate(AXES):
            b = 128 * h
            c[h, "o", 1] = copies(row(2, b, 64), o.at[h, 0], neighbour(first, 1))
            c[h, "o", 3] = copies(row(2, b + 64, 64), o.at[h, 1], neighbour(first, 3))
            c[h, "e", 1] = copies(row(1, b + 64, 64), n.at[h, 0, pl.ds(64, 64)], neighbour(first, 1))
            c[h, "e", 3] = copies(row(3, b, 64), n.at[h, 1, pl.ds(0, 64)], neighbour(first, 3))
            c[h, "l", 1] = copies(row(1, b, 64), n.at[h, 0, pl.ds(0, 64)], neighbour(first, 1))
            c[h, "l", 3] = copies(row(3, b + 64, 64), n.at[h, 1, pl.ds(64, 64)], neighbour(first, 3))
            c[h, "p", 1] = copies(row(0, b + 64, 16), o2.at[h, 0], neighbour(second, 1))
            c[h, "p", 3] = copies(row(0, b + 80, 16), o2.at[h, 1], neighbour(second, 3))
            c[h, "q", 1] = copies(row(0, b + 32, 32), n2.at[h, 0], neighbour(second, 1))
            c[h, "q", 3] = copies(row(0, b + 96, 32), n2.at[h, 1], neighbour(second, 3))

    def opposite(self):
        for h in (0, 1):
            self.c[h, "o", 1].start()
            self.c[h, "o", 3].start()

    def early(self, way):
        for h in (0, 1):
            self.c[h, "e", way].start()

    def step(self, number):
        c, row, width = self.c, self.row, self.width
        for h in (0, 1):
            b = 128 * h
            if number == 1:
                c[h, "o", 1].wait_recv()
                add_into(row(1, b, 64), [self.o.at[h, 0]], 64, width)
                c[h, "l", 1].start()
                c[h, "o", 3].wait_recv()
                add_into(row(3, b + 64, 64), [self.o.at[h, 1]], 64, width)
                c[h, "l", 3].start()
            elif number == 2:
                for way in (1, 3):
                    c[h, "e", way].wait_recv()
                    c[h, "l", way].wait_recv()
                add_into(row(0, b, 128), [self.n.at[h, 0], self.n.at[h, 1]], 128, width)
                c[h, "p", 1].start()
                c[h, "p", 3].start()
            elif number == 3:
                c[h, "p", 1].wait_recv()
                add_into(row(0, b + 32, 16), [self.o2.at[h, 0]], 16, width)
                c[h, "q", 1].start()
                c[h, "p", 3].wait_recv()
                add_into(row(0, b + 112, 16), [self.o2.at[h, 1]], 16, width)
                c[h, "q", 3].start()
            else:
                c[h, "q", 1].wait_recv()
                c[h, "q", 3].wait_recv()

    def total(self, h, cols):
        own = self.row(0, 128 * h, 32)[:, cols].astype(F32)
        return own + self.n2[h, 0, :, cols].astype(F32) + self.n2[h, 1, :, cols].astype(F32)

    def sent(self):
        for copy in self.c.values():
            copy.wait_send()


def kernel(
    ids, slots, weights, tokens, big_gate, big_up, big_down, small_gate, small_up, small_down,
    out,
    pk, dr, hm, xg, wgu, wd, hid, ob, nb, o2b, n2b, rb,
    sr, sc, sg, su, sd, ps, osm, ns, o2s, n2s, ah, back, sb,
    send, recv, local, tile_sem,
):
    width = tokens.shape[1]
    hidden = wd.shape[0]
    small = sg.shape[1]
    blocks = width // TILE
    half = width // 2
    e = lax.axis_index("expert")
    t = lax.axis_index("tensor")
    z, x = lax.div(t, 4), lax.rem(t, 4)

    def place(sz, sx):
        return lax.rem(z + sz, 4) * 4 + lax.rem(x + sx, 4)

    def peer(sz, sx):
        return {"tensor": place(sz, sx)}

    def neighbour(axis, s):
        return peer(s, 0) if axis == "z" else peer(0, s)

    offsets = [(sz, sx) for sz in range(4) for sx in range(4) if (sz, sx) != (0, 0)]

    barrier = pltpu.get_barrier_semaphore()
    for s in range(1, 8):
        pl.semaphore_signal(barrier, inc=1, device_id={"expert": lax.rem(e + s, 8)}, device_id_type=MESH)
    for sz, sx in offsets:
        pl.semaphore_signal(barrier, inc=1, device_id=peer(sz, sx), device_id_type=MESH)

    loads = [
        pltpu.make_async_copy(src, dst, local.at[k])
        for k, (src, dst) in enumerate(
            ((small_gate, sg), (small_up, su), (big_down, wd), (small_down, sd))
        )
    ]
    for load in loads:
        load.start()

    def tile_loads(j, slot):
        cols = pl.ds(pl.multiple_of(j * 128, 128), 128)
        return (
            pltpu.make_async_copy(big_gate.at[:, cols], wgu.at[slot, :, pl.ds(0, 128)], tile_sem.at[slot, 0]),
            pltpu.make_async_copy(big_up.at[:, cols], wgu.at[slot, :, pl.ds(128, 128)], tile_sem.at[slot, 1]),
        )

    for load in tile_loads(0, 0):
        load.start()

    where = (ids[...] & 7) * 16 + (ids[...] >> 3) * 8 + slots[...]
    spot = lax.broadcasted_iota(jnp.int32, (128, tokens.shape[0]), 0)
    first, second = spot == where[0:1, :], spot == where[1:2, :]
    onehot = (first.astype(F32) + second.astype(F32)).astype(BF16)

    @pl.loop(0, blocks)
    def _(c):
        cols = pl.ds(pl.multiple_of(c * TILE, TILE), TILE)
        rows = jnp.dot(onehot, tokens[:, cols], preferred_element_type=F32)
        pk[:, :, cols] = rows.astype(BF16).reshape(8, 16, TILE)

    pl.semaphore_wait(barrier, 22)

    copies = Copies(send, recv)
    dispatch = []
    for s in range(1, 8):
        to = lax.rem(e + s, 8)
        dispatch.append(copies(pk.at[to], dr.at[e], {"expert": to}))
    for copy in dispatch:
        copy.start()
    dr[e] = pk[e]

    out_row = lax.broadcasted_iota(jnp.int32, (128, 128), 0)
    in_row = lax.broadcasted_iota(jnp.int32, (128, 128), 1)
    from_row = ((out_row & 63) >> 3) * 16 + (out_row >> 6) * 8 + (out_row & 7)
    by_kind = (from_row == in_row).astype(F32).astype(BF16)
    back_row = (in_row & 63) >> 3
    back_row = back_row * 16 + (in_row >> 6) * 8 + (in_row & 7)
    by_group = (back_row == out_row).astype(F32).astype(BF16)

    for copy in dispatch:
        copy.wait_recv()

    @pl.loop(0, blocks)
    def _(c):
        cols = pl.ds(pl.multiple_of(c * TILE, TILE), TILE)
        rows = dr[:, :, cols].reshape(128, TILE)
        rows = jnp.dot(by_kind, rows, preferred_element_type=F32).astype(BF16)
        xg[0, 0:32, cols] = rows[0:32]
        xg[0, 128:160, cols] = rows[32:64]
        sr[c] = rows[64:128]

    columns = []
    for sz, sx in offsets:
        rel = (-sz) % 4 * 4 + (-sx) % 4
        columns.append(copies(sr.at[place(sz, sx)], sc.at[rel], peer(sz, sx)))
    for copy in columns:
        copy.start()
    sc[0] = sr[t]

    gather = Gather(copies, neighbour, xg)
    gather.step(0)
    gather.step(1)

    small_sum = Scatter(
        copies, neighbour, lambda g, lo, n: ps.at[g, pl.ds(lo, n)], 2 * small, osm, ns, o2s, n2s
    )

    def small_terms(g):
        rows = jnp.concatenate(
            [sc[4 * g + r, 0:32] for r in range(4)] + [sc[4 * r + g, 32:64] for r in range(4)], axis=0
        )

        @pl.loop(0, small // TILE)
        def _(c):
            cols = pl.ds(pl.multiple_of(c * TILE, TILE), TILE)
            far = pl.ds(pl.multiple_of(small + c * TILE, TILE), TILE)
            ps[g, :, cols] = jnp.dot(rows, sg[:, cols], preferred_element_type=F32).astype(BF16)
            ps[g, :, far] = jnp.dot(rows, su[:, cols], preferred_element_type=F32).astype(BF16)

    for load in loads[:2]:
        load.wait()
    for copy in columns:
        copy.wait_recv()
    small_terms(2)
    small_sum.opposite()
    gather.step(2)
    small_terms(1)
    small_sum.early(1)
    small_terms(3)
    small_sum.early(3)
    gather.step(3)
    small_terms(0)
    gather.step(4)
    gather.step(5)
    small_sum.step(1)
    gather.step(6)

    def big_hidden(lo, hi):
        @pl.loop(lo, hi)
        def _(j):
            slot = lax.rem(j, 2)
            for load in tile_loads(j, slot):
                load.wait()

            @pl.when(j + 1 < hidden // 128)
            def _():
                for load in tile_loads(j + 1, 1 - slot):
                    load.start()

            cols = pl.ds(pl.multiple_of(j * 128, 128), 128)

            @pl.loop(0, 4)
            def _(g):
                both = jnp.dot(xg[g], wgu[slot], preferred_element_type=F32)
                gate, up = both[:, :128], both[:, 128:]
                hid[g, :, cols] = (gate / (1.0 + jnp.exp(-gate)) * up).astype(BF16)

    tiles = hidden // 128
    marks = [0, tiles * 2 // 7, tiles * 4 // 7, tiles * 6 // 7, tiles]
    big_hidden(marks[0], marks[1])
    small_sum.step(2)
    big_hidden(marks[1], marks[2])
    small_sum.step(3)
    big_hidden(marks[2], marks[3])
    small_sum.step(4)

    for h in (0, 1):
        @pl.loop(0, small // TILE)
        def _(c):
            cols = pl.ds(pl.multiple_of(c * TILE, TILE), TILE)
            far = pl.ds(pl.multiple_of(small + c * TILE, TILE), TILE)
            gate, up = small_sum.total(h, cols), small_sum.total(h, far)
            ah[0, pl.ds(128 * h, 32), cols] = (gate / (1.0 + jnp.exp(-gate)) * up).astype(BF16)

    act = Gather(copies, neighbour, ah)
    act.step(0)
    big_hidden(marks[3], marks[4])
    act.step(1)

    gather.sent()
    loads[2].wait()

    def big_terms(g, q):
        @pl.loop(q * half // TILE, (q + 1) * half // TILE)
        def _(c):
            cols = pl.ds(pl.multiple_of(c * TILE, TILE), TILE)
            xg[g, :, cols] = jnp.dot(hid[g], wd[:, cols], preferred_element_type=F32).astype(BF16)

    def big_scatter(q):
        def row(g, lo, n):
            return xg.at[g, pl.ds(lo, n), pl.ds(q * half, half)]

        return Scatter(copies, neighbour, row, half, ob.at[q], nb.at[q], o2b.at[q], n2b.at[q])

    sums = []
    for q in (0, 1):
        sums.append(big_scatter(q))
        big_terms(2, q)
        sums[q].opposite()
        big_terms(1, q)
        sums[q].early(1)
        big_terms(3, q)
        sums[q].early(3)
        big_terms(0, q)
        act.step(2 + 2 * q)
        act.step(3 + 2 * q)

    sums[0].step(1)
    act.step(6)
    loads[3].wait()
    for g in range(4):
        rows = jnp.dot(ah[g], sd[...], preferred_element_type=F32).astype(BF16)
        for r in range(4):
            back[4 * g + r, 0:32] = rows[32 * r:32 * r + 32]
            back[4 * r + g, 32:64] = rows[128 + 32 * r:160 + 32 * r]
    home = []
    for sz, sx in offsets:
        home.append(copies(back.at[4 * sz + sx], sb.at[t], peer(sz, sx)))
    for copy in home:
        copy.start()
    sb[t] = back[0]

    sums[1].step(1)
    for number in (2, 3, 4):
        for q in (0, 1):
            sums[q].step(number)
    for q in (0, 1):
        for h in (0, 1):
            @pl.loop(0, half // TILE)
            def _(c):
                cols = pl.ds(pl.multiple_of(c * TILE, TILE), TILE)
                far = pl.ds(pl.multiple_of(q * half + c * TILE, TILE), TILE)
                rb[pl.ds(32 * h, 32), far] = sums[q].total(h, cols).astype(BF16)

    for copy in home:
        copy.wait_recv()
    for copy in dispatch:
        copy.wait_send()

    @pl.loop(0, blocks)
    def _(c):
        cols = pl.ds(pl.multiple_of(c * TILE, TILE), TILE)
        rows = jnp.concatenate([rb[:, cols], sb[c]], axis=0)
        rows = jnp.dot(by_group, rows, preferred_element_type=F32).astype(BF16)
        pk[:, :, cols] = rows.reshape(8, 16, TILE)

    returned = []
    for s in range(1, 8):
        to = lax.rem(e + s, 8)
        returned.append(copies(pk.at[to], hm.at[e], {"expert": to}))
    for copy in returned:
        copy.start()
    hm[e] = pk[e]

    mix = jnp.where(first, weights[0:1, :], 0.0) + jnp.where(second, weights[1:2, :], 0.0)
    mix = mix.T
    coarse = mix.astype(BF16)
    fine = (mix - coarse.astype(F32)).astype(BF16)

    for copy in returned:
        copy.wait_recv()

    @pl.loop(0, blocks)
    def _(c):
        cols = pl.ds(pl.multiple_of(c * TILE, TILE), TILE)
        rows = hm[:, :, cols].reshape(128, TILE)
        total = jnp.dot(coarse, rows, preferred_element_type=F32)
        total += jnp.dot(fine, rows, preferred_element_type=F32)
        out[:, cols] = total.astype(BF16)

    for copy in columns + home + returned:
        copy.wait_send()
    for group in (small_sum, act, sums[0], sums[1]):
        group.sent()


def shards(
    tokens, expert_ids, slots, combine_weights,
    big_gate, big_up, big_down, small_gate, small_up, small_down,
):
    tok, width = tokens.shape
    hidden = big_gate.shape[2]
    small = small_gate.shape[2]
    half = width // 2
    vmem = pl.BlockSpec(memory_space=pltpu.VMEM)
    hbm = pl.BlockSpec(memory_space=pl.ANY)

    def buf(*shape):
        return pltpu.VMEM(shape, BF16)

    n_copies = 7 + 15 + 32 + 20 + 32 + 40 + 15 + 7
    return pl.pallas_call(
        kernel,
        out_shape=jax.ShapeDtypeStruct((tok, width), BF16),
        in_specs=[vmem] * 4 + [hbm] * 6,
        out_specs=vmem,
        scratch_shapes=[
            buf(8, 16, width), buf(8, 16, width), buf(8, 16, width),
            buf(4, 256, width), buf(2, width, 256), buf(hidden, width), buf(4, 256, hidden),
            buf(2, 2, 2, 64, half), buf(2, 2, 2, 128, half), buf(2, 2, 2, 16, half), buf(2, 2, 2, 32, half),
            buf(64, width),
            buf(16, 64, TILE), buf(16, 64, TILE),
            buf(TILE, small), buf(TILE, small), buf(small, TILE),
            buf(4, 256, 2 * small),
            buf(2, 2, 64, 2 * small), buf(2, 2, 128, 2 * small), buf(2, 2, 16, 2 * small), buf(2, 2, 32, 2 * small),
            buf(4, 256, small), buf(16, 64, TILE), buf(16, 64, TILE),
            pltpu.SemaphoreType.DMA((n_copies,)),
            pltpu.SemaphoreType.DMA((n_copies,)),
            pltpu.SemaphoreType.DMA((4,)),
            pltpu.SemaphoreType.DMA((2, 2)),
        ],
        compiler_params=pltpu.CompilerParams(
            collective_id=0, has_side_effects=True, vmem_limit_bytes=62 * 1024 * 1024
        ),
        cost_estimate=pl.CostEstimate(
            flops=6 * 1024 * width * hidden + 6 * 1024 * TILE * small,
            bytes_accessed=6 * width * hidden + 6 * TILE * small,
            transcendentals=1024 * hidden,
        ),
        name="moe_layer",
    )(
        expert_ids.T, slots.T, combine_weights.T, tokens,
        big_gate[0], big_up[0], big_down[0], small_gate[0], small_up[0], small_down[0],
    )


def solution(mesh):
    return jax.shard_map(
        shards,
        mesh=mesh,
        in_specs=(
            P(("expert", "tensor"), None),
            P(("expert", "tensor"), None),
            P(("expert", "tensor"), None),
            P(("expert", "tensor"), None),
            P("expert", None, "tensor"),
            P("expert", None, "tensor"),
            P("expert", "tensor", None),
            P("expert", "tensor", None),
            P("expert", "tensor", None),
            P("expert", None, "tensor"),
        ),
        out_specs=P(("expert", "tensor"), None),
        check_vma=False,
    )
```

time: 360 us -> 211 us (0.59)
  waiting for transfers between devices: 228 us -> 0 us
  Pallas kernels: 0 us -> 209 us
  blocking collectives: 56.4 us -> 0 us
  matrix products: 48.5 us -> 0 us
  between operations: 13.3 us -> 0.01 us
  starting transfers between devices: 6.45 us -> 0 us
  other arithmetic: 3.83 us -> 0 us
    pallas_call x0 -> x1, Pallas kernels: none -> 209 us  [shards(): pl.pallas_call(kernel, out_shape=jax.ShapeDtypeStruct((tok, width), BF16)...]
    psum x1 -> x0, waiting for transfers between devices: 99.3 us -> none  [shards(): lax.psum(up_part.astype(jnp.bfloat16), 'tensor').astype(jnp.float32)]
    reduce_scatter x1 -> x0, waiting for transfers between devices: 66.2 us -> none  [shards(): lax.psum_scatter(partial_value.astype(jnp.bfloat16), 'tensor', scatter_di...]
    all_to_all x3 -> x0, blocking collectives: 56.4 us -> none  [the longest x1 20.8 us: shards(): lax.all_to_all(packed, 'expert', split_axis=1, concat_axis=1, tiled=True)]
    dot_general x7 -> x0, matrix products: 48.5 us -> none  [the longest x1 12.5 us: shards(): up = jnp.dot(rows, big_up[0], preferred_element_type=jnp.float32)]
    all_gather x1 -> x0, waiting for transfers between devices: 47.5 us -> none  [shards(): lax.all_gather(received[0].reshape(groups * capacity, width), 'tensor', a...]
    all_to_all x1 -> x0, waiting for transfers between devices: 15.1 us -> none  [shards(): lax.all_to_all(outgoing, 'expert', split_axis=1, concat_axis=1, tiled=True)]
    all_to_all x1 -> x0, starting transfers between devices: 6.18 us -> none  [shards(): lax.all_to_all(outgoing, 'expert', split_axis=1, concat_axis=1, tiled=True)]
  transfers between devices with their start and end apart: 4 -> 0, of which waited for: 4 -> 0; matrix products, arithmetic and copies ran while one was open for 13% -> 0% of each run, Pallas kernels for 0% -> 0%
where the time goes in v1:
time: 211 us; the launch traced here: 210 us
  Pallas kernels  209 us (99%)
    pallas_call x1, Pallas kernels, shards(): pl.pallas_call(kernel, out_shape=jax.ShapeDtypeStruct((tok, width), BF16)...  209 us

profile of v1, /device:TPU:1, one launch (start us, length us, event | category | flops | bytes accessed | tf_op | source)
XLA Modules:
  0.0 210.4 jit_solution(17874628880228612565)
XLA Ops:
  0.0 208.8 %moe_layer.1 = bf16[32,4096]{1,0:T(8,128)(2,1)} custom-call(s32[2,32]{1,0:T(2,128)} %bitcast.15, s32[2,32]{1,0:T(2,128)} %bitcast.16, f32[2,32]{1,0:T(2,128)} %bitcast.17, bf16[32,4096]{1,0:T(8,128)(2,1)} %tokens.1, bf16[4096,896]{1,0:T(8,128)(2,1)} %bitcast.9, bf16[4096,896]{1,0:T(8,128)(2,1)} %bitcast.10, bf16[896,4096]{1,0:T(8,128)(2,1)} %bitcast.11, ...), custom_call_target="tpu_custom_call" | custom-call | flops 25367150592 | bytes 24772608 | tf_op jit(solution)/shard_map/moe_layer/pallas_call | solution.py:460
  208.8 1.7 copy.12

commit v2 on v1

v2 whole, which is shorter than its diff:
```python
import jax
import jax.numpy as jnp
from jax import lax
from jax.experimental import pallas as pl
from jax.experimental.pallas import tpu as pltpu
from jax.sharding import PartitionSpec as P

F32, BF16 = jnp.float32, jnp.bfloat16
MESH = pl.DeviceIdType.MESH
TILE = 256
AXES = (("x", "z"), ("z", "x"))


def add_into(dst, parts, rows, width):
    step = min(width, 512)

    @pl.loop(0, width // step)
    def _(c):
        cols = pl.ds(pl.multiple_of(c * step, step), step)
        total = dst[:, cols].astype(F32)
        for part in parts:
            total += part[:, cols].astype(F32)
        dst[:, cols] = total.astype(BF16)


class Copies:
    def __init__(self, send, recv):
        self.send, self.recv, self.used = send, recv, 0

    def __call__(self, src, dst, device):
        k = self.used
        self.used += 1
        return pltpu.make_async_remote_copy(
            src_ref=src, dst_ref=dst, send_sem=self.send.at[k], recv_sem=self.recv.at[k],
            device_id=device, device_id_type=MESH,
        )


class Gather:
    def __init__(self, copies, neighbour, buf):
        self.c = c = {}
        for h, (first, second) in enumerate(AXES):
            def row(g, r, lo=0, n=32):
                return buf.at[g, pl.ds(128 * h + 32 * r + lo, n)]

            c[h, "a", 1] = copies(row(0, 0), row(0, 3), neighbour(first, 1))
            c[h, "a", 3] = copies(row(0, 0), row(0, 1), neighbour(first, 3))
            c[h, "f", 1] = copies(row(0, 3, 0, 16), row(0, 2, 0, 16), neighbour(first, 1))
            c[h, "f", 3] = copies(row(0, 1, 16, 16), row(0, 2, 16, 16), neighbour(first, 3))
            for r in range(4):
                c[h, "b", 1, r] = copies(row(0, r), row(3, r), neighbour(second, 1))
                c[h, "b", 3, r] = copies(row(0, r), row(1, r), neighbour(second, 3))
            for r in (0, 1):
                c[h, "g", 1, r] = copies(row(3, r), row(2, r), neighbour(second, 1))
            for r in (2, 3):
                c[h, "g", 3, r] = copies(row(1, r), row(2, r), neighbour(second, 3))

    def step(self, number):
        c = self.c
        for h in (0, 1):
            def go(*keys):
                for key in keys:
                    c[(h, *key)].start()

            def got(*keys):
                for key in keys:
                    c[(h, *key)].wait_recv()

            if number == 0:
                go(("a", 1), ("a", 3), ("b", 1, 0), ("b", 3, 0))
            elif number == 1:
                got(("a", 1))
                go(("f", 1), ("b", 1, 3), ("b", 3, 3))
                got(("a", 3))
                go(("f", 3), ("b", 1, 1), ("b", 3, 1))
            elif number == 2:
                got(("b", 1, 0))
                go(("g", 1, 0))
            elif number == 3:
                got(("f", 1), ("f", 3))
                go(("b", 1, 2), ("b", 3, 2))
            elif number == 4:
                got(("b", 1, 1))
                go(("g", 1, 1))
                got(("b", 3, 3))
                go(("g", 3, 3))
            elif number == 5:
                got(("b", 3, 2))
                go(("g", 3, 2))
            elif number == 6:
                got(("b", 1, 2), ("b", 1, 3), ("b", 3, 0), ("b", 3, 1))
            else:
                got(("g", 1, 0), ("g", 1, 1), ("g", 3, 2), ("g", 3, 3))

    def sent(self, relayed):
        for key, copy in self.c.items():
            if (key[1] == "g") == relayed:
                copy.wait_send()


class LineGather:
    def __init__(self, copies, neighbour, axis, buf, own=None):
        middle = buf.shape[1] // 2
        low, high = pl.ds(0, middle), pl.ds(middle, middle)
        up, down = neighbour(axis, 1), neighbour(axis, 3)
        own = buf.at[0] if own is None else own
        self.out = [copies(own, buf.at[3], up), copies(own, buf.at[1], down)]
        self.on = [
            copies(buf.at[3, low], buf.at[2, low], up), copies(buf.at[1, high], buf.at[2, high], down)
        ]

    def start(self):
        for copy in self.out:
            copy.start()

    def relay(self):
        for first, second in zip(self.out, self.on):
            first.wait_recv()
            second.start()

    def finish(self):
        for copy in self.on:
            copy.wait_recv()

    def sent(self):
        for copy in self.out + self.on:
            copy.wait_send()


class LineScatter:
    def __init__(self, copies, neighbour, axis, buf, o, n):
        low, high = pl.ds(0, 128), pl.ds(128, 128)
        up, down = neighbour(axis, 1), neighbour(axis, 3)
        self.buf, self.o, self.n = buf, o, n
        self.low, self.high = low, high
        self.far = [copies(buf.at[2, low], o.at[0], up), copies(buf.at[2, high], o.at[1], down)]
        self.early = [copies(buf.at[1, high], n.at[0, high], up), copies(buf.at[3, low], n.at[1, low], down)]
        self.late = [copies(buf.at[1, low], n.at[0, low], up), copies(buf.at[3, high], n.at[1, high], down)]

    def relay(self):
        width = self.o.shape[-1]
        self.far[0].wait_recv()
        add_into(self.buf.at[1, self.low], [self.o.at[0]], 128, width)
        self.late[0].start()
        self.far[1].wait_recv()
        add_into(self.buf.at[3, self.high], [self.o.at[1]], 128, width)
        self.late[1].start()

    def finish(self):
        for copy in self.early + self.late:
            copy.wait_recv()

    def total(self, cols):
        return self.buf[0, :, cols].astype(F32) + self.n[0, :, cols].astype(F32) + self.n[1, :, cols].astype(F32)

    def sent(self):
        for copy in self.far + self.early + self.late:
            copy.wait_send()


class Scatter:
    def __init__(self, copies, neighbour, row, width, o, n, o2, n2):
        self.row, self.width = row, width
        self.o, self.n, self.o2, self.n2 = o, n, o2, n2
        self.c = c = {}
        for h, (second, first) in enumerate(AXES):
            b = 128 * h
            c[h, "o", 1] = copies(row(2, b, 64), o.at[h, 0], neighbour(first, 1))
            c[h, "o", 3] = copies(row(2, b + 64, 64), o.at[h, 1], neighbour(first, 3))
            c[h, "e", 1] = copies(row(1, b + 64, 64), n.at[h, 0, pl.ds(64, 64)], neighbour(first, 1))
            c[h, "e", 3] = copies(row(3, b, 64), n.at[h, 1, pl.ds(0, 64)], neighbour(first, 3))
            c[h, "l", 1] = copies(row(1, b, 64), n.at[h, 0, pl.ds(0, 64)], neighbour(first, 1))
            c[h, "l", 3] = copies(row(3, b + 64, 64), n.at[h, 1, pl.ds(64, 64)], neighbour(first, 3))
            c[h, "p", 1] = copies(row(0, b + 64, 16), o2.at[h, 0], neighbour(second, 1))
            c[h, "p", 3] = copies(row(0, b + 80, 16), o2.at[h, 1], neighbour(second, 3))
            c[h, "q", 1] = copies(row(0, b + 32, 32), n2.at[h, 0], neighbour(second, 1))
            c[h, "q", 3] = copies(row(0, b + 96, 32), n2.at[h, 1], neighbour(second, 3))

    def opposite(self):
        for h in (0, 1):
            self.c[h, "o", 1].start()
            self.c[h, "o", 3].start()

    def early(self, way):
        for h in (0, 1):
            self.c[h, "e", way].start()

    def step(self, number):
        c, row, width = self.c, self.row, self.width
        for h in (0, 1):
            b = 128 * h
            if number == 1:
                c[h, "o", 1].wait_recv()
                add_into(row(1, b, 64), [self.o.at[h, 0]], 64, width)
                c[h, "l", 1].start()
                c[h, "o", 3].wait_recv()
                add_into(row(3, b + 64, 64), [self.o.at[h, 1]], 64, width)
                c[h, "l", 3].start()
            elif number == 2:
                for way in (1, 3):
                    c[h, "e", way].wait_recv()
                    c[h, "l", way].wait_recv()
                add_into(row(0, b, 128), [self.n.at[h, 0], self.n.at[h, 1]], 128, width)
                c[h, "p", 1].start()
                c[h, "p", 3].start()
            elif number == 3:
                c[h, "p", 1].wait_recv()
                add_into(row(0, b + 32, 16), [self.o2.at[h, 0]], 16, width)
                c[h, "q", 1].start()
                c[h, "p", 3].wait_recv()
                add_into(row(0, b + 112, 16), [self.o2.at[h, 1]], 16, width)
                c[h, "q", 3].start()
            else:
                c[h, "q", 1].wait_recv()
                c[h, "q", 3].wait_recv()

    def total(self, h, cols):
        own = self.row(0, 128 * h, 32)[:, cols].astype(F32)
        return own + self.n2[h, 0, :, cols].astype(F32) + self.n2[h, 1, :, cols].astype(F32)

    def sent(self):
        for copy in self.c.values():
            copy.wait_send()


def kernel(
    ids, slots, weights, tokens, big_gate, big_up, big_down, small_gate, small_up, small_down,
    out,
    pk, dr, hm, xg, wgu, wd, hid, ob, nb, o2b, n2b,
    sr, xs, wg, wu, wo, ps, op, np_, ac, pd, sb,
    send, recv, local, tile_sem,
):
    width = tokens.shape[1]
    hidden = wd.shape[0]
    tiles = hidden // 128
    blocks = width // TILE
    half = width // 2
    e = lax.axis_index("expert")
    t = lax.axis_index("tensor")
    z, x = lax.div(t, 4), lax.rem(t, 4)

    def peer(sz, sx):
        return {"tensor": lax.rem(z + sz, 4) * 4 + lax.rem(x + sx, 4)}

    def neighbour(axis, s):
        return peer(s, 0) if axis == "z" else peer(0, s)

    barrier = pltpu.get_barrier_semaphore()
    for s in range(1, 8):
        pl.semaphore_signal(barrier, inc=1, device_id={"expert": lax.rem(e + s, 8)}, device_id_type=MESH)
    for s in range(1, 4):
        for axis in ("x", "z"):
            pl.semaphore_signal(barrier, inc=1, device_id=neighbour(axis, s), device_id_type=MESH)

    def units(place):
        return pl.multiple_of(128 * (4 * place - lax.max(place - 1, 0)), 128)

    mine = pl.ds(units(x), 512)
    loads = [
        pltpu.make_async_copy(src, dst, local.at[k])
        for k, (src, dst) in enumerate((
            (small_gate.at[:, mine], wg.at[x]), (small_up.at[:, mine], wu.at[x]),
            (small_down, wo.at[0]), (big_down, wd),
        ))
    ]
    tile_loads = []
    for j in range(tiles):
        cols = pl.ds(j * 128, 128)
        tile_loads.append(pltpu.make_async_copy(big_gate.at[:, cols], wgu.at[j, :, pl.ds(0, 128)], tile_sem.at[j, 0]))
        tile_loads.append(pltpu.make_async_copy(big_up.at[:, cols], wgu.at[j, :, pl.ds(128, 128)], tile_sem.at[j, 1]))
    for load in loads + tile_loads:
        load.start()

    where = (ids[...] & 7) * 16 + (ids[...] >> 3) * 8 + slots[...]
    spot = lax.broadcasted_iota(jnp.int32, (128, tokens.shape[0]), 0)
    first, second = spot == where[0:1, :], spot == where[1:2, :]
    onehot = (first.astype(F32) + second.astype(F32)).astype(BF16)

    @pl.loop(0, blocks)
    def _(c):
        cols = pl.ds(pl.multiple_of(c * TILE, TILE), TILE)
        rows = jnp.dot(onehot, tokens[:, cols], preferred_element_type=F32)
        pk[:, :, cols] = rows.astype(BF16).reshape(8, 16, TILE)

    pl.semaphore_wait(barrier, 13)

    copies = Copies(send, recv)
    dispatch = []
    for s in range(1, 8):
        to = lax.rem(e + s, 8)
        dispatch.append(copies(pk.at[to], dr.at[e], {"expert": to}))
    for copy in dispatch:
        copy.start()
    shared = []
    for src, dst in ((small_gate, wg), (small_up, wu)):
        for s in range(1, 4):
            theirs = pl.ds(units(lax.rem(x + s, 4)), 512)
            shared.append(copies(src.at[:, theirs], dst.at[x], peer(0, s)))
    for copy in shared:
        copy.start()
    down_in = LineGather(copies, neighbour, "z", wo, small_down)
    down_in.start()
    dr[e] = pk[e]

    out_row = lax.broadcasted_iota(jnp.int32, (128, 128), 0)
    in_row = lax.broadcasted_iota(jnp.int32, (128, 128), 1)
    by_kind = ((out_row & 63) >> 3) * 16 + (out_row >> 6) * 8 + (out_row & 7) == in_row
    by_group = ((in_row & 63) >> 3) * 16 + (in_row >> 6) * 8 + (in_row & 7) == out_row
    by_kind, by_group = by_kind.astype(F32).astype(BF16), by_group.astype(F32).astype(BF16)

    for copy in dispatch:
        copy.wait_recv()

    @pl.loop(0, blocks)
    def _(c):
        cols = pl.ds(pl.multiple_of(c * TILE, TILE), TILE)
        inner = pl.ds(pl.multiple_of(lax.rem(c, 4) * TILE, TILE), TILE)
        rows = dr[:, :, cols].reshape(128, TILE)
        rows = jnp.dot(by_kind, rows, preferred_element_type=F32).astype(BF16)
        xg[0, 0:32, cols] = rows[0:32]
        xg[0, 128:160, cols] = rows[32:64]
        sr[lax.div(c, 4), :, inner] = rows[64:128]

    gather = Gather(copies, neighbour, xg)
    gather.step(0)
    spread = []
    for s in range(1, 4):
        spread.append(copies(sr.at[lax.rem(z + s, 4)], xs.at[0, pl.ds(64 * (4 - s), 64)], peer(s, 0)))
    for copy in spread:
        copy.start()
    xs[0, 0:64] = sr[z]

    rows_in = LineGather(copies, neighbour, "x", xs)
    terms_in = LineScatter(copies, neighbour, "z", ps, op, np_)
    acts = LineGather(copies, neighbour, "x", ac)

    def big_scatter(q):
        def row(g, lo, n):
            return xg.at[g, pl.ds(lo, n), pl.ds(q * half, half)]

        return Scatter(copies, neighbour, row, half, ob.at[q], nb.at[q], o2b.at[q], n2b.at[q])

    sums = [big_scatter(0), big_scatter(1)]

    def big_hidden(g, lo, hi):
        @pl.loop(lo, hi)
        def _(j):
            cols = pl.ds(pl.multiple_of(j * 128, 128), 128)
            both = jnp.dot(xg[g], wgu[j], preferred_element_type=F32)
            gate, up = both[:, :128], both[:, 128:]
            hid[g, :, cols] = (gate / (1.0 + jnp.exp(-gate)) * up).astype(BF16)

    def big_terms(g, q):
        @pl.loop(q * half // TILE, (q + 1) * half // TILE)
        def _(c):
            cols = pl.ds(pl.multiple_of(c * TILE, TILE), TILE)
            xg[g, :, cols] = jnp.dot(hid[g], wd[:, cols], preferred_element_type=F32).astype(BF16)

    def small_terms(g):
        rows = jnp.concatenate([xs[r, 64 * g:64 * g + 64] for r in range(4)], axis=0)

        @pl.loop(0, 2)
        def _(c):
            cols = pl.ds(pl.multiple_of(c * TILE, TILE), TILE)
            far = pl.ds(pl.multiple_of(512 + c * TILE, TILE), TILE)
            ps[g, :, cols] = jnp.dot(
                rows, wg[:, :, cols].reshape(1024, TILE), preferred_element_type=F32).astype(BF16)
            ps[g, :, far] = jnp.dot(
                rows, wu[:, :, cols].reshape(1024, TILE), preferred_element_type=F32).astype(BF16)

    def small_hidden():
        @pl.loop(0, 4)
        def _(c):
            cols = pl.ds(pl.multiple_of(c * 128, 128), 128)
            far = pl.ds(pl.multiple_of(512 + c * 128, 128), 128)
            gate, up = terms_in.total(cols), terms_in.total(far)
            act = gate / (1.0 + jnp.exp(-gate)) * up
            twice = jnp.logical_and(c == 0, x >= 2)
            act = jnp.where(twice, 0.0, act).astype(BF16)
            for r in range(4):
                here = pl.ds(pl.multiple_of(lax.rem(x + r, 4) * 64, 64), 64)
                ac[0, here, cols] = act[64 * r:64 * r + 64]

    def small_back():
        @pl.loop(0, 4)
        def _(c):
            rows = jnp.zeros((256, TILE), F32)
            for k in range(4):
                some = pl.ds(units(lax.rem(x + k, 4)), 512)
                rows += jnp.dot(ac[k], wo[c, some, :], preferred_element_type=F32)
            cols = pl.ds(pl.multiple_of(c * TILE, TILE), TILE)
            pd[:, :, cols] = rows.astype(BF16).reshape(4, 64, TILE)

    gather.step(1)
    for copy in spread:
        copy.wait_recv()
    rows_in.start()
    gather.step(2)
    gather.step(3)
    for load in tile_loads:
        load.wait()
    big_hidden(0, 0, 3)
    gather.step(4)
    rows_in.relay()
    big_hidden(0, 3, tiles)
    gather.step(5)
    down_in.relay()
    rows_in.finish()
    for load in loads[:2]:
        load.wait()
    for copy in shared:
        copy.wait_recv()
    small_terms(2)
    for copy in terms_in.far:
        copy.start()
    small_terms(1)
    terms_in.early[0].start()
    small_terms(3)
    terms_in.early[1].start()
    small_terms(0)
    gather.step(6)
    big_hidden(1, 0, tiles)
    terms_in.relay()
    big_hidden(3, 0, tiles)
    loads[3].wait()
    gather.sent(True)
    big_terms(1, 0)
    sums[0].early(1)
    big_terms(3, 0)
    sums[0].early(3)
    terms_in.finish()
    small_hidden()
    acts.start()
    gather.step(7)
    big_hidden(2, 0, tiles)
    big_terms(2, 0)
    sums[0].opposite()
    acts.relay()
    big_terms(2, 1)
    sums[1].opposite()
    big_terms(1, 1)
    sums[1].early(1)
    big_terms(3, 1)
    sums[1].early(3)
    gather.sent(False)
    sums[0].step(1)
    acts.finish()
    down_in.finish()
    loads[2].wait()
    small_back()
    home = []
    for s in range(1, 4):
        home.append(copies(pd.at[lax.rem(x + s, 4)], sb.at[x], peer(0, s)))
    for copy in home:
        copy.start()
    sb[x] = pd[x]
    big_terms(0, 0)
    big_terms(0, 1)
    sums[1].step(1)
    sums[0].step(2)
    sums[1].step(2)

    mix = jnp.where(first, weights[0:1, :], 0.0) + jnp.where(second, weights[1:2, :], 0.0)
    mix = mix.T
    coarse = mix.astype(BF16)
    fine = (mix - coarse.astype(F32)).astype(BF16)
    for copy in dispatch:
        copy.wait_send()

    returned = [[], []]
    for q in (0, 1):
        for s in range(1, 8):
            to = lax.rem(e + s, 8)
            part = pl.ds(q * half, half)
            returned[q].append(copies(pk.at[to, :, part], hm.at[e, :, part], {"expert": to}))

    sums[0].step(3)
    sums[1].step(3)
    for q in (0, 1):
        sums[q].step(4)
        if q == 0:
            for copy in home:
                copy.wait_recv()

        @pl.loop(0, half // TILE)
        def _(c):
            cols = pl.ds(pl.multiple_of(c * TILE, TILE), TILE)
            far = pl.ds(pl.multiple_of(q * half + c * TILE, TILE), TILE)
            steps = lax.rem(2 * q + lax.div(c, 4) - z + 4, 4)
            inner = pl.ds(pl.multiple_of(steps * TILE, TILE), TILE)
            rows = jnp.concatenate(
                [sums[q].total(h, cols).astype(BF16) for h in (0, 1)]
                + [sb[lax.rem(c, 4), :, inner]], axis=0)
            rows = jnp.dot(by_group, rows, preferred_element_type=F32).astype(BF16)
            pk[:, :, far] = rows.reshape(8, 16, TILE)

        for copy in returned[q]:
            copy.start()
        part = slice(q * half, (q + 1) * half)
        hm[e, :, part] = pk[e, :, part]

    for q in (0, 1):
        for copy in returned[q]:
            copy.wait_recv()

        @pl.loop(q * half // TILE, (q + 1) * half // TILE)
        def _(c):
            cols = pl.ds(pl.multiple_of(c * TILE, TILE), TILE)
            rows = hm[:, :, cols].reshape(128, TILE)
            total = jnp.dot(coarse, rows, preferred_element_type=F32)
            total += jnp.dot(fine, rows, preferred_element_type=F32)
            out[:, cols] = total.astype(BF16)

    for copy in shared + spread + home + returned[0] + returned[1]:
        copy.wait_send()
    for group in (down_in, rows_in, terms_in, acts, sums[0], sums[1]):
        group.sent()


def shards(
    tokens, expert_ids, slots, combine_weights,
    big_gate, big_up, big_down, small_gate, small_up, small_down,
):
    tok, width = tokens.shape
    hidden = big_gate.shape[2]
    small = small_gate.shape[2]
    half = width // 2
    vmem = pl.BlockSpec(memory_space=pltpu.VMEM)
    hbm = pl.BlockSpec(memory_space=pl.ANY)

    def buf(*shape):
        return pltpu.VMEM(shape, BF16)

    n_copies = 7 + 6 + 4 + 32 + 3 + 4 + 6 + 4 + 40 + 3 + 14
    return pl.pallas_call(
        kernel,
        out_shape=jax.ShapeDtypeStruct((tok, width), BF16),
        in_specs=[vmem] * 4 + [hbm] * 6,
        out_specs=vmem,
        scratch_shapes=[
            buf(8, 16, width), buf(8, 16, width), buf(8, 16, width),
            buf(4, 256, width), buf(hidden // 128, width, 256), buf(hidden, width), buf(4, 256, hidden),
            buf(2, 2, 2, 64, half), buf(2, 2, 2, 128, half), buf(2, 2, 2, 16, half), buf(2, 2, 2, 32, half),
            buf(4, 64, 1024), buf(4, 256, 1024), buf(4, 256, 512), buf(4, 256, 512), buf(4, small, 256),
            buf(4, 256, 1024), buf(2, 128, 1024), buf(2, 256, 1024),
            buf(4, 256, 512),
            buf(4, 64, 1024), buf(4, 64, 1024),
            pltpu.SemaphoreType.DMA((n_copies,)),
            pltpu.SemaphoreType.DMA((n_copies,)),
            pltpu.SemaphoreType.DMA((4,)),
            pltpu.SemaphoreType.DMA((hidden // 128, 2)),
        ],
        compiler_params=pltpu.CompilerParams(
            collective_id=0, has_side_effects=True, vmem_limit_bytes=62 * 1024 * 1024
        ),
        cost_estimate=pl.CostEstimate(
            flops=6 * 1024 * width * hidden + 6 * 1024 * TILE * small,
            bytes_accessed=6 * width * hidden + 6 * TILE * small,
            transcendentals=1024 * hidden,
        ),
        name="moe_layer",
    )(
        expert_ids.T, slots.T, combine_weights.T, tokens,
        big_gate[0], big_up[0], big_down[0], small_gate[0], small_up[0], small_down[0],
    )


def solution(mesh):
    return jax.shard_map(
        shards,
        mesh=mesh,
        in_specs=(
            P(("expert", "tensor"), None),
            P(("expert", "tensor"), None),
            P(("expert", "tensor"), None),
            P(("expert", "tensor"), None),
            P("expert", None, "tensor"),
            P("expert", None, "tensor"),
            P("expert", "tensor", None),
            P("expert", "tensor", None),
            P("expert", "tensor", None),
            P("expert", None, "tensor"),
        ),
        out_specs=P(("expert", "tensor"), None),
        check_vma=False,
    )
```

time: 211 us -> 185 us (0.88)
  Pallas kernels: 209 us -> 183 us
    pallas_call x1, Pallas kernels: 209 us -> 183 us  [shards(): pl.pallas_call(kernel, out_shape=jax.ShapeDtypeStruct((tok, width), BF16)...]
where the time goes in v2:
time: 185 us; the launch traced here: 184 us
  Pallas kernels  183 us (99%)
    pallas_call x1, Pallas kernels, shards(): pl.pallas_call(kernel, out_shape=jax.ShapeDtypeStruct((tok, width), BF16)...  183 us

profile of v2, /device:TPU:1, one launch (start us, length us, event | category | flops | bytes accessed | tf_op | source)
XLA Modules:
  0.0 184.4 jit_solution(1685406270354693532)
XLA Ops:
  0.0 182.7 %moe_layer.1 = bf16[32,4096]{1,0:T(8,128)(2,1)} custom-call(s32[2,32]{1,0:T(2,128)} %bitcast.15, s32[2,32]{1,0:T(2,128)} %bitcast.16, f32[2,32]{1,0:T(2,128)} %bitcast.17, bf16[32,4096]{1,0:T(8,128)(2,1)} %tokens.1, bf16[4096,896]{1,0:T(8,128)(2,1)} %bitcast.9, bf16[4096,896]{1,0:T(8,128)(2,1)} %bitcast.10, bf16[896,4096]{1,0:T(8,128)(2,1)} %bitcast.11, ...), custom_call_target="tpu_custom_call" | custom-call | flops 25367150592 | bytes 24772608 | tf_op jit(solution)/shard_map/moe_layer/pallas_call | solution.py:535
  182.7 1.7 copy.12

commit v3 on v2

--- a/solution.py
+++ b/solution.py
@@ -299,7 +299,6 @@
     for copy in shared:
         copy.start()
     down_in = LineGather(copies, neighbour, "z", wo, small_down)
-    down_in.start()
     dr[e] = pk[e]
 
     out_row = lax.broadcasted_iota(jnp.int32, (128, 128), 0)
@@ -397,14 +396,17 @@
     rows_in.start()
     gather.step(2)
     gather.step(3)
+    down_in.start()
     for load in tile_loads:
         load.wait()
+    loads[3].wait()
     big_hidden(0, 0, 3)
     gather.step(4)
-    rows_in.relay()
     big_hidden(0, 3, tiles)
     gather.step(5)
-    down_in.relay()
+    rows_in.relay()
+    gather.step(6)
+    big_hidden(1, 0, tiles)
     rows_in.finish()
     for load in loads[:2]:
         load.wait()
@@ -417,33 +419,35 @@
     terms_in.early[0].start()
     small_terms(3)
     terms_in.early[1].start()
+    gather.step(7)
+    big_hidden(2, 0, tiles)
+    gather.sent(True)
+    big_terms(2, 0)
+    sums[0].opposite()
+    big_terms(2, 1)
+    sums[1].opposite()
+    down_in.relay()
+    terms_in.relay()
     small_terms(0)
-    gather.step(6)
-    big_hidden(1, 0, tiles)
-    terms_in.relay()
-    big_hidden(3, 0, tiles)
-    loads[3].wait()
-    gather.sent(True)
     big_terms(1, 0)
     sums[0].early(1)
+    big_terms(1, 1)
+    sums[1].early(1)
+    big_hidden(3, 0, tiles)
     big_terms(3, 0)
     sums[0].early(3)
+    big_terms(3, 1)
+    sums[1].early(3)
     terms_in.finish()
     small_hidden()
     acts.start()
-    gather.step(7)
-    big_hidden(2, 0, tiles)
-    big_terms(2, 0)
-    sums[0].opposite()
+    sums[0].step(1)
+    sums[1].step(1)
+    gather.sent(False)
+    big_terms(0, 0)
     acts.relay()
-    big_terms(2, 1)
-    sums[1].opposite()
-    big_terms(1, 1)
-    sums[1].early(1)
-    big_terms(3, 1)
-    sums[1].early(3)
-    gather.sent(False)
-    sums[0].step(1)
+    big_terms(0, 1)
+    sums[0].step(2)
     acts.finish()
     down_in.finish()
     loads[2].wait()
@@ -454,11 +458,9 @@
     for copy in home:
         copy.start()
     sb[x] = pd[x]
-    big_terms(0, 0)
-    big_terms(0, 1)
-    sums[1].step(1)
-    sums[0].step(2)
     sums[1].step(2)
+    sums[0].step(3)
+    sums[1].step(3)
 
     mix = jnp.where(first, weights[0:1, :], 0.0) + jnp.where(second, weights[1:2, :], 0.0)
     mix = mix.T
@@ -474,8 +476,6 @@
             part = pl.ds(q * half, half)
             returned[q].append(copies(pk.at[to, :, part], hm.at[e, :, part], {"expert": to}))
 
-    sums[0].step(3)
-    sums[1].step(3)
     for q in (0, 1):
         sums[q].step(4)
         if q == 0:

time: 185 us -> 184 us (level)
  no operation moved by 1% of the time
where the time goes in v3:
time: 184 us
  Pallas kernels  183 us (99%)
    pallas_call x1, Pallas kernels, shards(): pl.pallas_call(kernel, out_shape=jax.ShapeDtypeStruct((tok, width), BF16)...  183 us

profile of v3, /device:TPU:1, one launch (start us, length us, event | category | flops | bytes accessed | tf_op | source)
XLA Modules:
  0.0 184.3 jit_solution(14435515260045962235)
XLA Ops:
  0.0 182.6 %moe_layer.1 = bf16[32,4096]{1,0:T(8,128)(2,1)} custom-call(s32[2,32]{1,0:T(2,128)} %bitcast.15, s32[2,32]{1,0:T(2,128)} %bitcast.16, f32[2,32]{1,0:T(2,128)} %bitcast.17, bf16[32,4096]{1,0:T(8,128)(2,1)} %tokens.1, bf16[4096,896]{1,0:T(8,128)(2,1)} %bitcast.9, bf16[4096,896]{1,0:T(8,128)(2,1)} %bitcast.10, bf16[896,4096]{1,0:T(8,128)(2,1)} %bitcast.11, ...), custom_call_target="tpu_custom_call" | custom-call | flops 25367150592 | bytes 24772608 | tf_op jit(solution)/shard_map/moe_layer/pallas_call | solution.py:535
  182.6 1.7 copy.12
